TPU v7x, 512 devices: a whole 4x8x8 slice. The times are simulated.
512 devices in a mesh: leaf: 128 (over z, y, core), sub: 4 (over x).
Axes of the slice: x: 4, y: 8, z: 8, core: 2. Of those that a mesh axis runs over, the one named last changes fastest.
Arguments:
- light: bfloat16 [32, 1048576], P(None, ('leaf', 'sub')), may hold values from -6 to 6
- probes: bfloat16 [4, 1048576], P(None, ('leaf', 'sub')), may hold values from 0 to 1, as said below
- near_list: int32 [4096, 4], P(('leaf', 'sub')), may hold values from 0 to 4095, as said below
- far_list: int32 [4096, 32], P(('leaf', 'sub')), may hold values from 0 to 4095, as said below
- leaf_basis: bfloat16 [4096, 256, 64], P(('leaf', 'sub')), may hold values from -0.375 to 0.375
- leaf_transfer: bfloat16 [4096, 64, 64], P(('leaf', 'sub')), may hold values from -0.25 to 0.25
- far_coupling: bfloat16 [4096, 32, 64, 64], P(('leaf', 'sub')), may hold values from -0.125 to 0.125
- up_transfer: bfloat16 [3, 2, 64, 64], replicated, may hold values from -0.5 to 0.5
- upper_coupling: bfloat16 [4, 2, 64, 64], replicated, may hold values from -0.5 to 0.5
Outputs:
- irradiance: bfloat16 [32, 1048576], P(None, ('leaf', 'sub'))
Inputs may be any that keep to these rules, and one draw needn't show every extreme that they name: `near_list`: each leaf's list names 4 distinct leaves other than itself, each within 4 leaf numbers of it. `far_list`: every entry names a leaf on a device with the same sub index as the leaf's own device and another leaf index. The entries of one device's leaves name leaves of any one other device at most 4 times, and exactly 4 times for some device. `probes`: rows 0 to 2 lie in the unit box, row 3 is positive.
All inputs are finite; a program needn't handle non-finite values.
Results may differ from a plain program's by a relative error of at most 0.0049.
The roundings to bfloat16 on the way count: a program that leaves them out, or rounds other values in their place, can miss the bound.
Values may be sent and summed in bfloat16 or wider, within the bound.
A program may use at most 128 MiB of HBM per device.

v0:
```python
import jax
import jax.numpy as jnp
from jax import lax
from jax.sharding import PartitionSpec as P

HALO = 4
UPLV = 3
soften = 0.0025
spacing = 0.25


def extended(value, sides, width):
    for axis, dim in sides:
        size, length = (lax.axis_size(axis), value.shape[dim])
        up = [(i, (i + 1) % size) for i in range(size - 1)]
        down = [(j, i) for i, j in up]
        last = lax.slice_in_dim(value, length - width, length, axis=dim)
        leading = lax.slice_in_dim(value, 0, width, axis=dim)
        before = lax.ppermute(last, axis, up)
        after = lax.ppermute(leading, axis, down)
        value = jnp.concatenate([before, value, after], axis=dim)
    return value


def from_partner(value, axis, distance):
    mask = 2**distance
    pairs = [(source, source ^ mask) for source in range(lax.axis_size(axis))]
    return lax.ppermute(value, axis, pairs)


def passed_along(value, axis, steps):
    count = lax.axis_size(axis)
    leading, last = (max(0, -steps), min(count, count - steps))
    return lax.ppermute(value, axis, [(source, source + steps) for source in range(leading, last)])


def kernel_block(target_geo, source_geo, offset):
    delta_x = target_geo[0][:, None] - source_geo[0][None, :] + spacing * offset
    delta_y = target_geo[1][:, None] - source_geo[1][None, :]
    delta_z = target_geo[2][:, None] - source_geo[2][None, :]
    square = delta_x * delta_x + delta_y * delta_y + delta_z * delta_z
    return target_geo[3][:, None] * source_geo[3][None, :] * (soften / (soften + square))


def high_product(left_matrix, right_matrix):
    return jnp.dot(left_matrix, right_matrix.astype(jnp.float32), precision=lax.Precision.HIGHEST)


def high_transposed(left_matrix, right_matrix):
    return lax.dot_general(
        left_matrix,
        right_matrix.astype(jnp.float32),
        (((1,), (1,)), ((), ())),
        precision=lax.Precision.HIGHEST,
    )


def per_device(
    light,
    probes,
    near_list,
    far_list,
    leaf_basis,
    leaf_transfer,
    far_coupling,
    up_transfer,
    upper_coupling,
):
    leaf_count = leaf_basis.shape[0]
    leaf_size = leaf_basis.shape[1]
    rank_size = leaf_basis.shape[2]
    light_rows = light.shape[0]
    device_index = lax.axis_index(("leaf", "sub"))
    anchor = device_index * leaf_count
    stacked = jnp.concatenate([light, probes], axis=0)
    padded = extended(stacked, ((("leaf", "sub"), 1),), HALO * leaf_size)
    local_ids = anchor + jnp.arange(leaf_count, dtype=jnp.int32)
    target_geo = probes.astype(jnp.float32).reshape(4, leaf_count, leaf_size)
    tile_maker = jax.vmap(kernel_block, in_axes=(1, 1, None))
    near_terms = jnp.zeros((light_rows, leaf_count, leaf_size), jnp.float32)
    for step in range(-HALO, HALO + 1):
        start = (HALO + step) * leaf_size
        window = padded[:, start : start + leaf_count * leaf_size]
        source_values = window[:light_rows].reshape(light_rows, leaf_count, leaf_size)
        source_geo = window[light_rows:].astype(jnp.float32).reshape(4, leaf_count, leaf_size)
        kernel_tiles = tile_maker(target_geo, source_geo, jnp.float32(-step)).astype(jnp.bfloat16)
        contribution = jnp.einsum(
            "rjl,jil->rji", source_values, kernel_tiles, preferred_element_type=jnp.float32
        )
        if step == 0:
            near_terms = near_terms + contribution
        else:
            chosen = jnp.any(near_list == (local_ids + step)[:, None], axis=1).astype(jnp.float32)
            near_terms = near_terms + contribution * chosen[None, :, None]
    light_blocks = light.reshape(light_rows, leaf_count, leaf_size)
    coefficients = jnp.einsum(
        "rjl,jlk->jrk", light_blocks, leaf_basis, preferred_element_type=jnp.float32
    ).astype(jnp.bfloat16)
    coeff_flat = coefficients.reshape(leaf_count, light_rows * rank_size)
    entries = far_list.reshape(-1)
    groups = lax.axis_size("sub")
    peer_row = entries // leaf_count // groups
    which_leaf = entries % leaf_count
    pooled = lax.all_gather(coeff_flat, "leaf", axis=0, tiled=True)
    picked = pooled[peer_row * leaf_count + which_leaf]
    picked = picked.reshape(leaf_count, -1, light_rows, rank_size)
    far_terms = jnp.einsum(
        "jcrk,jckm->jrm", picked, far_coupling, preferred_element_type=jnp.float32
    )
    upward = [
        jnp.einsum("jrk,jkm->rm", coefficients, leaf_transfer, preferred_element_type=jnp.float32)
    ]
    for height in range(UPLV):
        parity = device_index >> height & 1
        mine_term = high_product(upward[-1], up_transfer[height][parity])
        other_term = from_partner(mine_term, ("leaf", "sub"), height)
        left_term = jnp.where(parity == 0, mine_term, other_term)
        right_term = jnp.where(parity == 0, other_term, mine_term)
        upward.append(left_term + right_term)
    downward = None
    for height in range(UPLV, -1, -1):
        stride = 2 ** (height + 1)
        lower_part = passed_along(upward[height], ("leaf", "sub"), stride)
        upper_part = passed_along(upward[height], ("leaf", "sub"), -stride)
        coupled = high_product(lower_part, upper_coupling[height, 0]) + high_product(
            upper_part, upper_coupling[height, 1]
        )
        if downward is not None:
            parity = device_index >> height & 1
            coupled = coupled + high_transposed(downward, up_transfer[height][parity])
        downward = coupled
    pulled = jnp.einsum(
        "rk,jmk->jrm", downward, leaf_transfer.astype(jnp.float32), precision=lax.Precision.HIGHEST
    )
    leaf_far = (far_terms + pulled).astype(jnp.bfloat16)
    spread = jnp.einsum("jrk,jlk->rjl", leaf_far, leaf_basis, preferred_element_type=jnp.float32)
    combined = near_terms + spread
    return combined.reshape(light_rows, leaf_count * leaf_size).astype(jnp.bfloat16)


def solution(mesh):
    return jax.shard_map(
        per_device,
        mesh=mesh,
        in_specs=(
            P(None, ("leaf", "sub")),
            P(None, ("leaf", "sub")),
            P(("leaf", "sub"), None),
            P(("leaf", "sub"), None),
            P(("leaf", "sub"), None, None),
            P(("leaf", "sub"), None, None),
            P(("leaf", "sub"), None, None, None),
            P(),
            P(),
        ),
        out_specs=P(None, ("leaf", "sub")),
        check_vma=False,
    )
```

profile of v0, /device:TPU:1, one launch (start us, length us, event | category | flops | bytes accessed | tf_op | source)
XLA Modules:
  0.0 131.3 jit_solution(11800955980936551876)
XLA Ops:
  7.5 1.1 convolution_convert_fusion
  8.6 1.1 convolution_bitcast_fusion.3
  9.7 6.0 %collective-permute-start.3 = (f32[32,64]{1,0:T(8,128)S(1)}, f32[32,64]{1,0:T(8,128)S(1)}, u32[]{:S(2)}, u32[]{:S(2)}) collective-permute-start(f32[32,64]{1,0:T(8,128)S(1)} %convolution_bitcast_fusion.3), channel_id=1, source_target_pairs={{2,0},{3,1},{4,2},{5,3},{6,4},{7,5},{8,6},{9,7},{10,8},{11,9},{12,... | collective-permute-start | bytes 24584 | tf_op jit(solution)/shard_map/ppermute | solution.py:34
  15.7 1.9 %collective-permute-start.2 = (f32[32,64]{1,0:T(8,128)S(1)}, f32[32,64]{1,0:T(8,128)S(1)}, u32[]{:S(2)}, u32[]{:S(2)}) collective-permute-start(f32[32,64]{1,0:T(8,128)S(1)} %convolution_bitcast_fusion.3), channel_id=1, source_target_pairs={{0,2},{1,3},{2,4},{3,5},{4,6},{5,7},{6,8},{7,9},{8,10},{9,11},{10,... | collective-permute-start | bytes 24584 | tf_op jit(solution)/shard_map/ppermute | solution.py:34
  18.6 2.8 %collective-permute-start.4 = (f32[32,64]{1,0:T(8,128)S(1)}, f32[32,64]{1,0:T(8,128)S(1)}, u32[]{:S(2)}, u32[]{:S(2)}) collective-permute-start(f32[32,64]{1,0:T(8,128)S(1)} %fusion.154), channel_id=1, source_target_pairs={{0,1},{1,0},{2,3},{3,2},{4,5},{5,4},{6,7},{7,6},{8,9},{9,8},{10,11... | collective-permute-start | bytes 24584 | tf_op jit(solution)/shard_map/ppermute | solution.py:28
  23.9 2.5 %collective-permute-start = (bf16[36,1024]{1,0:T(8,128)(2,1)S(1)}, bf16[36,1024]{1,0:T(8,128)(2,1)S(1)}, u32[]{:S(2)}, u32[]{:S(2)}) collective-permute-start(bf16[36,1024]{1,0:T(8,128)(2,1)S(1)} %get-tuple-element.74), channel_id=1, source_target_pairs={{0,1},{1,2},{2,3},{3,4},{4,5},{5,6},{6,7},{7,8},{8,9},{9,10},{10,1... | collective-permute-start | bytes 221192 | tf_op jit(solution)/shard_map/ppermute | solution.py:19
  26.4 6.9 %collective-permute-start.1 = (bf16[36,1024]{1,0:T(8,128)(2,1)S(1)}, bf16[36,1024]{1,0:T(8,128)(2,1)S(1)}, u32[]{:S(2)}, u32[]{:S(2)}) collective-permute-start(bf16[36,1024]{1,0:T(8,128)(2,1)S(1)} %get-tuple-element.73), channel_id=1, source_target_pairs={{1,0},{2,1},{3,2},{4,3},{5,4},{6,5},{7,6},{8,7},{9,8},{10,9},{11,1... | collective-permute-start | bytes 221192 | tf_op jit(solution)/shard_map/ppermute | solution.py:20
  35.2 3.1 %collective-permute-start.6 = (f32[32,64]{1,0:T(8,128)S(1)}, f32[32,64]{1,0:T(8,128)S(1)}, u32[]{:S(2)}, u32[]{:S(2)}) collective-permute-start(f32[32,64]{1,0:T(8,128)S(1)} %select_add_fusion.2), channel_id=1, source_target_pairs={{4,0},{5,1},{6,2},{7,3},{8,4},{9,5},{10,6},{11,7},{12,8},{13,9},{1... | collective-permute-start | bytes 24584 | tf_op jit(solution)/shard_map/ppermute | solution.py:34
  38.5 4.3 %collective-permute-start.7 = (f32[32,64]{1,0:T(8,128)S(1)}, f32[32,64]{1,0:T(8,128)S(1)}, u32[]{:S(2)}, u32[]{:S(2)}) collective-permute-start(f32[32,64]{1,0:T(8,128)S(1)} %fusion.147), channel_id=1, source_target_pairs={{0,2},{1,3},{2,0},{3,1},{4,6},{5,7},{6,4},{7,5},{8,10},{9,11},{10,... | collective-permute-start | bytes 24584 | tf_op jit(solution)/shard_map/ppermute | solution.py:28
  42.9 1.7 %collective-permute-done.7 = f32[32,64]{1,0:T(8,128)S(1)} collective-permute-done((f32[32,64]{1,0:T(8,128)S(1)}, f32[32,64]{1,0:T(8,128)S(1)}, u32[]{:S(2)}, u32[]{:S(2)}) %collective-permute-start.7) | collective-permute-done | bytes 8224 | tf_op jit(solution)/shard_map/ppermute | solution.py:28
  44.6 3.4 %collective-permute-start.5 = (f32[32,64]{1,0:T(8,128)S(1)}, f32[32,64]{1,0:T(8,128)S(1)}, u32[]{:S(2)}, u32[]{:S(2)}) collective-permute-start(f32[32,64]{1,0:T(8,128)S(1)} %select_add_fusion.2), channel_id=1, source_target_pairs={{0,4},{1,5},{2,6},{3,7},{4,8},{5,9},{6,10},{7,11},{8,12},{9,13},{1... | collective-permute-start | bytes 24584 | tf_op jit(solution)/shard_map/ppermute | solution.py:34
  48.2 1.9 %collective-permute-start.10 = (f32[32,64]{1,0:T(8,128)S(1)}, f32[32,64]{1,0:T(8,128)S(1)}, u32[]{:S(2)}, u32[]{:S(2)}) collective-permute-start(f32[32,64]{1,0:T(8,128)S(1)} %fusion.140), channel_id=1, source_target_pairs={{0,4},{1,5},{2,6},{3,7},{4,0},{5,1},{6,2},{7,3},{8,12},{9,13},{10,... | collective-permute-start | bytes 24584 | tf_op jit(solution)/shard_map/ppermute | solution.py:28
  50.2 1.0 collective-permute-done.10
  51.3 1.3 collective-permute-start.9
  52.6 3.6 %collective-permute-done.9 = f32[32,64]{1,0:T(8,128)S(1)} collective-permute-done((f32[32,64]{1,0:T(8,128)S(1)}, f32[32,64]{1,0:T(8,128)S(1)}, u32[]{:S(2)}, u32[]{:S(2)}) %collective-permute-start.9) | collective-permute-done | bytes 8224 | tf_op jit(solution)/shard_map/ppermute | solution.py:34
  56.2 1.3 collective-permute-start.12
  57.6 5.8 %collective-permute-done.12 = f32[32,64]{1,0:T(8,128)S(1)} collective-permute-done((f32[32,64]{1,0:T(8,128)S(1)}, f32[32,64]{1,0:T(8,128)S(1)}, u32[]{:S(2)}, u32[]{:S(2)}) %collective-permute-start.12) | collective-permute-done | bytes 8224 | tf_op jit(solution)/shard_map/ppermute | solution.py:34
  63.4 5.1 %collective-permute-start.11 = (f32[32,64]{1,0:T(8,128)S(1)}, f32[32,64]{1,0:T(8,128)S(1)}, u32[]{:S(2)}, u32[]{:S(2)}) collective-permute-start(f32[32,64]{1,0:T(8,128)S(1)} %select_add_fusion), channel_id=1, source_target_pairs={{0,16},{1,17},{2,18},{3,19},{4,20},{5,21},{6,22},{7,23},{8,24},{9,... | collective-permute-start | bytes 24584 | tf_op jit(solution)/shard_map/ppermute | solution.py:34
  69.3 4.5 %collective-permute-start.8 = (f32[32,64]{1,0:T(8,128)S(1)}, f32[32,64]{1,0:T(8,128)S(1)}, u32[]{:S(2)}, u32[]{:S(2)}) collective-permute-start(f32[32,64]{1,0:T(8,128)S(1)} %select_add_fusion.1), channel_id=1, source_target_pairs={{0,8},{1,9},{2,10},{3,11},{4,12},{5,13},{6,14},{7,15},{8,16},{9,17... | collective-permute-start | bytes 24584 | tf_op jit(solution)/shard_map/ppermute | solution.py:34
  76.6 2.7 %convolution_multiply_fusion.7 = f32[8,256,32]{1,2,0:T(8,128)S(1)} fusion(f32[8,256]{1,0:T(8,128)S(1)} %sub.188, f32[8,256]{1,0:T(8,128)S(1)} %sub.186, f32[8,256]{1,0:T(8,128)S(1)} %sub.183, f32[8,256]{1,0:T(8,128)S(1)} %sub.181, f32[8,256]{1,0:T(8,128)S(1)} %sub.178, f32[8,256]{1,0:T(8,128)S(1)} %sub.176, f32[8,256]{1,0:T(8,128)S(1)} %mul.326, ...), kind=kOutput, calls=%fused_computation.28 | convolution fusion | flops 40960000 | bytes 458784 | tf_op jit(solution)/shard_map/rjl,jil->rji/dot_general | solution.py:87
  79.3 2.6 %fusion.8 = f32[8,256,32]{1,2,0:T(8,128)S(1)} fusion(f32[8,256,32]{1,2,0:T(8,128)S(1)} %convolution_multiply_fusion.7, f32[8,256]{1,0:T(8,128)S(1)} %sub.388, f32[8,256]{1,0:T(8,128)S(1)} %sub.385, f32[8,256]{1,0:T(8,128)S(1)} %sub.382, f32[8,256]{1,0:T(8,128)S(1)} %mul.337, f32[8,256]{1,0:T(8,128)S(1)} %sub.186, f32[8,256]{1,0:T(8,128)S(1)} %sub.181, ...), kind=kOutput, calls=%fused_computation.27 | convolution fusion | flops 41025536 | bytes 720928 | tf_op jit(solution)/shard_map/rjl,jil->rji/dot_general | solution.py:87
  81.9 2.7 %fusion.7 = f32[8,256,32]{1,2,0:T(8,128)S(1)} fusion(f32[8,256,32]{1,2,0:T(8,128)S(1)} %fusion.8, f32[8,256]{1,0:T(8,128)S(1)} %sub.397, f32[8,256]{1,0:T(8,128)S(1)} %sub.394, f32[8,256]{1,0:T(8,128)S(1)} %sub.391, f32[8,256]{1,0:T(8,128)S(1)} %mul.346, f32[8,256]{1,0:T(8,128)S(1)} %sub.186, f32[8,256]{1,0:T(8,128)S(1)} %sub.181, f32[8,256]{1,0:T(8,128)S(1)} %sub.176, ...), kind=kOutput, calls=%fused_computation.25 | convolution fusion | flops 41025536 | bytes 720928 | tf_op jit(solution)/shard_map/rjl,jil->rji/dot_general | solution.py:87
  84.6 2.6 %fusion.6 = f32[8,256,32]{1,2,0:T(8,128)S(1)} fusion(f32[8,256,32]{1,2,0:T(8,128)S(1)} %fusion.7, f32[8,256]{1,0:T(8,128)S(1)} %sub.406, f32[8,256]{1,0:T(8,128)S(1)} %sub.403, f32[8,256]{1,0:T(8,128)S(1)} %sub.400, f32[8,256]{1,0:T(8,128)S(1)} %mul.355, f32[8,256]{1,0:T(8,128)S(1)} %sub.186, f32[8,256]{1,0:T(8,128)S(1)} %sub.181, f32[8,256]{1,0:T(8,128)S(1)} %sub.176, ...), kind=kOutput, calls=%fused_computation.23 | convolution fusion | flops 41025536 | bytes 720928 | tf_op jit(solution)/shard_map/rjl,jil->rji/dot_general | solution.py:87
  87.2 2.6 %convolution_add_fusion = f32[8,256,32]{1,2,0:T(8,128)S(1)} fusion(f32[8,256,32]{1,2,0:T(8,128)S(1)} %fusion.6, f32[8,256]{1,0:T(8,128)S(1)} %sub.186, f32[8,256]{1,0:T(8,128)S(1)} %sub.181, f32[8,256]{1,0:T(8,128)S(1)} %sub.176, f32[8,256]{1,0:T(8,128)S(1)} %mul.324, bf16[4,8,8,256]{3,2,1,0:T(8,128)(2,1)S(1)} %bitcast.128), kind=kOutput, calls=%fused_computation.21 | convolution fusion | flops 40435712 | bytes 688128 | tf_op jit(solution)/shard_map/rjl,jil->rji/dot_general | solution.py:87
  89.9 2.6 %fusion.5 = f32[8,256,32]{1,2,0:T(8,128)S(1)} fusion(f32[8,256,32]{1,2,0:T(8,128)S(1)} %convolution_add_fusion, f32[8,256]{1,0:T(8,128)S(1)} %sub.421, f32[8,256]{1,0:T(8,128)S(1)} %sub.418, f32[8,256]{1,0:T(8,128)S(1)} %sub.415, f32[8,256]{1,0:T(8,128)S(1)} %mul.370, f32[8,256]{1,0:T(8,128)S(1)} %sub.186, f32[8,256]{1,0:T(8,128)S(1)} %sub.181, ...), kind=kOutput, calls=%fused_computation.20 | convolution fusion | flops 41025536 | bytes 720928 | tf_op jit(solution)/shard_map/rjl,jil->rji/dot_general | solution.py:87
  92.5 2.6 %fusion.4 = f32[8,256,32]{1,2,0:T(8,128)S(1)} fusion(f32[8,256,32]{1,2,0:T(8,128)S(1)} %fusion.5, f32[8,256]{1,0:T(8,128)S(1)} %sub.430, f32[8,256]{1,0:T(8,128)S(1)} %sub.427, f32[8,256]{1,0:T(8,128)S(1)} %sub.424, f32[8,256]{1,0:T(8,128)S(1)} %mul.380, f32[8,256]{1,0:T(8,128)S(1)} %sub.186, f32[8,256]{1,0:T(8,128)S(1)} %sub.181, f32[8,256]{1,0:T(8,128)S(1)} %sub.176, ...), kind=kOutput, calls=%fused_computation.18 | convolution fusion | flops 41025536 | bytes 720928 | tf_op jit(solution)/shard_map/rjl,jil->rji/dot_general | solution.py:87
  95.1 2.6 %fusion.3 = f32[8,256,32]{1,2,0:T(8,128)S(1)} fusion(f32[8,256,32]{1,2,0:T(8,128)S(1)} %fusion.4, f32[8,256]{1,0:T(8,128)S(1)} %sub.439, f32[8,256]{1,0:T(8,128)S(1)} %sub.436, f32[8,256]{1,0:T(8,128)S(1)} %sub.433, f32[8,256]{1,0:T(8,128)S(1)} %mul.390, f32[8,256]{1,0:T(8,128)S(1)} %sub.186, f32[8,256]{1,0:T(8,128)S(1)} %sub.181, f32[8,256]{1,0:T(8,128)S(1)} %sub.176, ...), kind=kOutput, calls=%fused_computation.16 | convolution fusion | flops 41025536 | bytes 720928 | tf_op jit(solution)/shard_map/rjl,jil->rji/dot_general | solution.py:87
  97.8 2.7 %fusion.2 = f32[32,8,256]{2,0,1:T(8,128)} fusion(f32[8,256,32]{1,2,0:T(8,128)S(1)} %fusion.3, f32[8,256]{1,0:T(8,128)S(1)} %sub.448, f32[8,256]{1,0:T(8,128)S(1)} %sub.445, f32[8,256]{1,0:T(8,128)S(1)} %sub.442, f32[8,256]{1,0:T(8,128)S(1)} %mul.400, f32[8,256]{1,0:T(8,128)S(1)} %sub.186, f32[8,256]{1,0:T(8,128)S(1)} %sub.181, f32[8,256]{1,0:T(8,128)S(1)} %sub.176, ...), kind=kOutput, calls=%fused_computation.14 | convolution fusion | flops 41025536 | bytes 720928 | tf_op jit(solution)/shard_map/rjl,jil->rji/dot_general | solution.py:87
  100.5 12.3 %all-gather.2.cloned.1.call-done = bf16[1024,2048]{1,0:T(8,128)(2,1)} async-done(((bf16[8,2048]{1,0:T(8,128)(2,1)}), bf16[1024,2048]{1,0:T(8,128)(2,1)}) %all-gather.2.cloned.1.call-update) | async-done | bytes 4194320 | tf_op jit(solution)/shard_map/all_gather | solution.py:104
  112.8 5.1 %gather_fusion = bf16[256,2048]{1,0:T(8,128)(2,1)S(1)} fusion(bf16[1024,2048]{1,0:T(8,128)(2,1)} %all-gather.2.cloned.1.call-done, s32[1024]{0:T(1024)S(1)} %pad_clamp_fusion), kind=kCustom, calls=%fused_computation | custom fusion | bytes 2098176 | tf_op jit(solution)/shard_map/gather | solution.py:105
  117.9 2.2 %reshape.387 = bf16[8,32,32,64]{3,2,1,0:T(8,128)(2,1)S(1)} reshape(bf16[256,2048]{1,0:T(8,128)(2,1)S(1)} %gather_fusion) | data formatting | bytes 2097152 | tf_op jit(solution)/shard_map/reshape | solution.py:106
  120.1 3.0 %convolution_bitcast_fusion.1 = f32[8,32,64]{2,1,0:T(8,128)S(1)} fusion(bf16[8,32,32,64]{3,2,1,0:T(8,128)(2,1)S(1)} %reshape.387, bf16[8,32,64,64]{3,2,1,0:T(8,128)(2,1)} %param.15), kind=kOutput, calls=%fused_computation.31 | convolution fusion | flops 67108864 | bytes 3211264 | tf_op jit(solution)/shard_map/jcrk,jckm->jrm/dot_general | solution.py:107
  (105 shorter events, 11.3 us)
Async XLA Ops:
  6.5 1.0 copy-start
  6.5 36.3 %copy-start.4 = (bf16[4,2,64,64]{3,2,1,0:T(8,128)(2,1)S(1)}, bf16[4,2,64,64]{3,2,1,0:T(8,128)(2,1)}, u32[]{:S(2)}) copy-start(bf16[4,2,64,64]{3,2,1,0:T(8,128)(2,1)} %param.17) | copy-start | bytes 196612
  6.5 106.2 %all-gather.2.cloned.1.call-start = ((), (), s32[]{:S(2)}) async-start(), calls=%async_computation | async-start | bytes 4227072 | tf_op jit(solution)/shard_map/all_gather | solution.py:104
  9.7 28.8 %collective-permute-start.3 = (f32[32,64]{1,0:T(8,128)S(1)}, f32[32,64]{1,0:T(8,128)S(1)}, u32[]{:S(2)}, u32[]{:S(2)}) collective-permute-start(f32[32,64]{1,0:T(8,128)S(1)} %convolution_bitcast_fusion.3), channel_id=1, source_target_pairs={{2,0},{3,1},{4,2},{5,3},{6,4},{7,5},{8,6},{9,7},{10,8},{11,9},{12,... | collective-permute-start | bytes 24584 | tf_op jit(solution)/shard_map/ppermute | solution.py:34
  15.7 59.5 %collective-permute-start.2 = (f32[32,64]{1,0:T(8,128)S(1)}, f32[32,64]{1,0:T(8,128)S(1)}, u32[]{:S(2)}, u32[]{:S(2)}) collective-permute-start(f32[32,64]{1,0:T(8,128)S(1)} %convolution_bitcast_fusion.3), channel_id=1, source_target_pairs={{0,2},{1,3},{2,4},{3,5},{4,6},{5,7},{6,8},{7,9},{8,10},{9,11},{10,... | collective-permute-start | bytes 24584 | tf_op jit(solution)/shard_map/ppermute | solution.py:34
  18.6 16.5 %collective-permute-start.4 = (f32[32,64]{1,0:T(8,128)S(1)}, f32[32,64]{1,0:T(8,128)S(1)}, u32[]{:S(2)}, u32[]{:S(2)}) collective-permute-start(f32[32,64]{1,0:T(8,128)S(1)} %fusion.154), channel_id=1, source_target_pairs={{0,1},{1,0},{2,3},{3,2},{4,5},{5,4},{6,7},{7,6},{8,9},{9,8},{10,11... | collective-permute-start | bytes 24584 | tf_op jit(solution)/shard_map/ppermute | solution.py:28
  23.9 51.5 %collective-permute-start = (bf16[36,1024]{1,0:T(8,128)(2,1)S(1)}, bf16[36,1024]{1,0:T(8,128)(2,1)S(1)}, u32[]{:S(2)}, u32[]{:S(2)}) collective-permute-start(bf16[36,1024]{1,0:T(8,128)(2,1)S(1)} %get-tuple-element.74), channel_id=1, source_target_pairs={{0,1},{1,2},{2,3},{3,4},{4,5},{5,6},{6,7},{7,8},{8,9},{9,10},{10,1... | collective-permute-start | bytes 221192 | tf_op jit(solution)/shard_map/ppermute | solution.py:19
  26.4 49.0 %collective-permute-start.1 = (bf16[36,1024]{1,0:T(8,128)(2,1)S(1)}, bf16[36,1024]{1,0:T(8,128)(2,1)S(1)}, u32[]{:S(2)}, u32[]{:S(2)}) collective-permute-start(bf16[36,1024]{1,0:T(8,128)(2,1)S(1)} %get-tuple-element.73), channel_id=1, source_target_pairs={{1,0},{2,1},{3,2},{4,3},{5,4},{6,5},{7,6},{8,7},{9,8},{10,9},{11,1... | collective-permute-start | bytes 221192 | tf_op jit(solution)/shard_map/ppermute | solution.py:20
  35.2 13.0 %collective-permute-start.6 = (f32[32,64]{1,0:T(8,128)S(1)}, f32[32,64]{1,0:T(8,128)S(1)}, u32[]{:S(2)}, u32[]{:S(2)}) collective-permute-start(f32[32,64]{1,0:T(8,128)S(1)} %select_add_fusion.2), channel_id=1, source_target_pairs={{4,0},{5,1},{6,2},{7,3},{8,4},{9,5},{10,6},{11,7},{12,8},{13,9},{1... | collective-permute-start | bytes 24584 | tf_op jit(solution)/shard_map/ppermute | solution.py:34
  38.5 6.1 %collective-permute-start.7 = (f32[32,64]{1,0:T(8,128)S(1)}, f32[32,64]{1,0:T(8,128)S(1)}, u32[]{:S(2)}, u32[]{:S(2)}) collective-permute-start(f32[32,64]{1,0:T(8,128)S(1)} %fusion.147), channel_id=1, source_target_pairs={{0,2},{1,3},{2,0},{3,1},{4,6},{5,7},{6,4},{7,5},{8,10},{9,11},{10,... | collective-permute-start | bytes 24584 | tf_op jit(solution)/shard_map/ppermute | solution.py:28
  44.6 30.3 %collective-permute-start.5 = (f32[32,64]{1,0:T(8,128)S(1)}, f32[32,64]{1,0:T(8,128)S(1)}, u32[]{:S(2)}, u32[]{:S(2)}) collective-permute-start(f32[32,64]{1,0:T(8,128)S(1)} %select_add_fusion.2), channel_id=1, source_target_pairs={{0,4},{1,5},{2,6},{3,7},{4,8},{5,9},{6,10},{7,11},{8,12},{9,13},{1... | collective-permute-start | bytes 24584 | tf_op jit(solution)/shard_map/ppermute | solution.py:34
  48.2 3.1 %collective-permute-start.10 = (f32[32,64]{1,0:T(8,128)S(1)}, f32[32,64]{1,0:T(8,128)S(1)}, u32[]{:S(2)}, u32[]{:S(2)}) collective-permute-start(f32[32,64]{1,0:T(8,128)S(1)} %fusion.140), channel_id=1, source_target_pairs={{0,4},{1,5},{2,6},{3,7},{4,0},{5,1},{6,2},{7,3},{8,12},{9,13},{10,... | collective-permute-start | bytes 24584 | tf_op jit(solution)/shard_map/ppermute | solution.py:28
  51.3 4.9 %collective-permute-start.9 = (f32[32,64]{1,0:T(8,128)S(1)}, f32[32,64]{1,0:T(8,128)S(1)}, u32[]{:S(2)}, u32[]{:S(2)}) collective-permute-start(f32[32,64]{1,0:T(8,128)S(1)} %select_add_fusion.1), channel_id=1, source_target_pairs={{8,0},{9,1},{10,2},{11,3},{12,4},{13,5},{14,6},{15,7},{16,8},{17,9... | collective-permute-start | bytes 24584 | tf_op jit(solution)/shard_map/ppermute | solution.py:34
  56.2 7.2 %collective-permute-start.12 = (f32[32,64]{1,0:T(8,128)S(1)}, f32[32,64]{1,0:T(8,128)S(1)}, u32[]{:S(2)}, u32[]{:S(2)}) collective-permute-start(f32[32,64]{1,0:T(8,128)S(1)} %select_add_fusion), channel_id=1, source_target_pairs={{16,0},{17,1},{18,2},{19,3},{20,4},{21,5},{22,6},{23,7},{24,8},{25... | collective-permute-start | bytes 24584 | tf_op jit(solution)/shard_map/ppermute | solution.py:34
  63.4 5.9 %collective-permute-start.11 = (f32[32,64]{1,0:T(8,128)S(1)}, f32[32,64]{1,0:T(8,128)S(1)}, u32[]{:S(2)}, u32[]{:S(2)}) collective-permute-start(f32[32,64]{1,0:T(8,128)S(1)} %select_add_fusion), channel_id=1, source_target_pairs={{0,16},{1,17},{2,18},{3,19},{4,20},{5,21},{6,22},{7,23},{8,24},{9,... | collective-permute-start | bytes 24584 | tf_op jit(solution)/shard_map/ppermute | solution.py:34
  69.3 5.4 %collective-permute-start.8 = (f32[32,64]{1,0:T(8,128)S(1)}, f32[32,64]{1,0:T(8,128)S(1)}, u32[]{:S(2)}, u32[]{:S(2)}) collective-permute-start(f32[32,64]{1,0:T(8,128)S(1)} %select_add_fusion.1), channel_id=1, source_target_pairs={{0,8},{1,9},{2,10},{3,11},{4,12},{5,13},{6,14},{7,15},{8,16},{9,17... | collective-permute-start | bytes 24584 | tf_op jit(solution)/shard_map/ppermute | solution.py:34
  84.6 2.6 %copy-start.1 = (bf16[32,2048]{1,0:T(8,128)(2,1)S(1)}, bf16[32,2048]{1,0:T(8,128)(2,1)}, u32[]{:S(2)}) copy-start(bf16[32,2048]{1,0:T(8,128)(2,1)} %param.9) | copy-start | bytes 393220
  120.1 3.1 %copy-start.2 = (bf16[8,64,64]{2,1,0:T(8,128)(2,1)S(1)}, bf16[8,64,64]{2,1,0:T(8,128)(2,1)}, u32[]{:S(2)}) copy-start(bf16[8,64,64]{2,1,0:T(8,128)(2,1)} %param.14) | copy-start | bytes 196612
  120.1 3.5 %copy-start.3 = (f32[32,8,256]{2,0,1:T(8,128)S(1)}, f32[32,8,256]{2,0,1:T(8,128)}, u32[]{:S(2)}) copy-start(f32[32,8,256]{2,0,1:T(8,128)} %fusion.2) | copy-start | bytes 786436
Sparse Core Ops, SparseCore 0:
  22.3 90.4 all-gather.1
where the time goes:
time: 132 us; the launch traced here: 131 us
  starting transfers between devices  45.1 us (34%)
  matrix products  31.5 us (24%)
  waiting for transfers between devices  25.8 us (20%)
  between operations  14.2 us (11%)
  local copies, waits for them, and re-layouts  13.1 us (10%)
  other arithmetic  1.75 us (1%)
    ppermute x8, starting transfers between devices, passed_along(): lax.ppermute(value, axis, [(source, source + steps) for source in range(l...  26.6 us
    dot_general x9, matrix products, per_device(): jnp.einsum('rjl,jil->rji', source_values, kernel_tiles, preferred_element...  23.8 us
    all_gather x1, waiting for transfers between devices, per_device(): pooled = lax.all_gather(coeff_flat, 'leaf', axis=0, tiled=True)  12.3 us
    ppermute x8, waiting for transfers between devices, passed_along(): lax.ppermute(value, axis, [(source, source + steps) for source in range(l...  10.8 us
    ppermute x3, starting transfers between devices, from_partner(): return lax.ppermute(value, axis, pairs)  9.02 us
    ppermute x1, starting transfers between devices, extended(): after = lax.ppermute(leading, axis, down)  6.9 us
    gather x1, local copies, waits for them, and re-layouts, per_device(): picked = pooled[peer_row * leaf_count + which_leaf]  5.09 us
    dot_general x1, matrix products, per_device(): jnp.einsum('jcrk,jckm->jrm', picked, far_coupling, preferred_element_type...  3.03 us
  transfers between devices with their start and end apart: 14, of which 7 were waited for; matrix products, arithmetic and copies ran while one was open for 24% of the time, Pallas kernels for 0%

commit v1 on v0

--- a/solution.py
+++ b/solution.py
@@ -101,7 +101,9 @@
     groups = lax.axis_size("sub")
     peer_row = entries // leaf_count // groups
     which_leaf = entries % leaf_count
-    pooled = lax.all_gather(coeff_flat, "leaf", axis=0, tiled=True)
+    pooled = jnp.concatenate(
+        lax.all_to_all(jnp.stack([coeff_flat] * lax.axis_size("leaf"), 0), "leaf", 0, 0), 0
+    )
     picked = pooled[peer_row * leaf_count + which_leaf]
     picked = picked.reshape(leaf_count, -1, light_rows, rank_size)
     far_terms = jnp.einsum(

time: 132 us -> 204 us (1.55)
  the two profiles are of different devices: /device:TPU:1 before, /device:TPU:256 now
where the time goes in v1:
time: 204 us; the launch traced here: 203 us
  waiting for transfers between devices  89.2 us (44%)
  starting transfers between devices  68.3 us (33%)
  matrix products  31.5 us (15%)
  local copies, waits for them, and re-layouts  13.4 us (7%)
    ppermute x8, waiting for transfers between devices, passed_along(): lax.ppermute(value, axis, [(source, source + steps) for source in range(l...  83.4 us
    ppermute x8, starting transfers between devices, passed_along(): lax.ppermute(value, axis, [(source, source + steps) for source in range(l...  31.5 us
    dot_general x9, matrix products, per_device(): jnp.einsum('rjl,jil->rji', source_values, kernel_tiles, preferred_element...  23.8 us
    all_to_all x1, starting transfers between devices, per_device(): lax.all_to_all(jnp.stack([coeff_flat] * lax.axis_size('leaf'), 0), 'leaf'...  14.7 us
    ppermute x3, starting transfers between devices, from_partner(): return lax.ppermute(value, axis, pairs)  11 us
    ppermute x1, starting transfers between devices, extended(): after = lax.ppermute(leading, axis, down)  8.55 us
    ppermute x3, waiting for transfers between devices, from_partner(): return lax.ppermute(value, axis, pairs)  5.77 us
    gather x1, local copies, waits for them, and re-layouts, per_device(): picked = pooled[peer_row * leaf_count + which_leaf]  5.09 us
  transfers between devices with their start and end apart: 14, of which 7 were waited for; matrix products, arithmetic and copies ran while one was open for 15% of the time, Pallas kernels for 0%

profile of v1, /device:TPU:256, one launch (start us, length us, event | category | flops | bytes accessed | tf_op | source)
XLA Modules:
  0.0 203.4 jit_solution(7602880766279877615)
XLA Ops:
  3.2 6.4 %collective-permute-start.3 = (f32[32,64]{1,0:T(8,128)S(1)}, f32[32,64]{1,0:T(8,128)S(1)}, u32[]{:S(2)}, u32[]{:S(2)}) collective-permute-start(f32[32,64]{1,0:T(8,128)S(1)} %convolution_bitcast_fusion.3), channel_id=1, source_target_pairs={{2,0},{3,1},{4,2},{5,3},{6,4},{7,5},{8,6},{9,7},{10,8},{11,9},{12,... | collective-permute-start | bytes 24584 | tf_op jit(solution)/shard_map/ppermute | solution.py:34
  9.5 1.9 collective-permute-start.2
  12.4 2.5 %collective-permute-start.4 = (f32[32,64]{1,0:T(8,128)S(1)}, f32[32,64]{1,0:T(8,128)S(1)}, u32[]{:S(2)}, u32[]{:S(2)}) collective-permute-start(f32[32,64]{1,0:T(8,128)S(1)} %fusion.154), channel_id=1, source_target_pairs={{0,1},{1,0},{2,3},{3,2},{4,5},{5,4},{6,7},{7,6},{8,9},{9,8},{10,11... | collective-permute-start | bytes 24584 | tf_op jit(solution)/shard_map/ppermute | solution.py:28
  15.0 2.5 %stack.3 = bf16[128,8,2048]{2,1,0:T(8,128)(2,1)} broadcast(bf16[8,2048]{1,0:T(8,128)(2,1)S(1)} %stack_reshape.2), dimensions={1,2} | broadcast | bytes 4227072 | tf_op jit(solution)/shard_map/stack | solution.py:105
  17.6 14.7 %all-to-all-start = ((bf16[128,8,2048]{2,1,0:T(8,128)(2,1)}), bf16[128,8,2048]{2,1,0:T(8,128)(2,1)}, u32[]{:S(2)}, u32[]{:S(2)}) async-start(bf16[128,8,2048]{2,1,0:T(8,128)(2,1)} %stack.3), calls=%async_computation | async-start | bytes 8388608 | tf_op jit(solution)/shard_map/all_to_all | solution.py:105
  32.4 2.4 %collective-permute-start = (bf16[36,1024]{1,0:T(8,128)(2,1)S(1)}, bf16[36,1024]{1,0:T(8,128)(2,1)S(1)}, u32[]{:S(2)}, u32[]{:S(2)}) collective-permute-start(bf16[36,1024]{1,0:T(8,128)(2,1)S(1)} %get-tuple-element.74), channel_id=1, source_target_pairs={{0,1},{1,2},{2,3},{3,4},{4,5},{5,6},{6,7},{7,8},{8,9},{9,10},{10,1... | collective-permute-start | bytes 221192 | tf_op jit(solution)/shard_map/ppermute | solution.py:19
  34.8 8.5 %collective-permute-start.1 = (bf16[36,1024]{1,0:T(8,128)(2,1)S(1)}, bf16[36,1024]{1,0:T(8,128)(2,1)S(1)}, u32[]{:S(2)}, u32[]{:S(2)}) collective-permute-start(bf16[36,1024]{1,0:T(8,128)(2,1)S(1)} %get-tuple-element.73), channel_id=1, source_target_pairs={{1,0},{2,1},{3,2},{4,3},{5,4},{6,5},{7,6},{8,7},{9,8},{10,9},{11,1... | collective-permute-start | bytes 221192 | tf_op jit(solution)/shard_map/ppermute | solution.py:20
  43.9 1.9 collective-permute-start.6
  46.0 1.9 collective-permute-start.7
  48.0 5.1 %collective-permute-done.7 = f32[32,64]{1,0:T(8,128)S(1)} collective-permute-done((f32[32,64]{1,0:T(8,128)S(1)}, f32[32,64]{1,0:T(8,128)S(1)}, u32[]{:S(2)}, u32[]{:S(2)}) %collective-permute-start.7) | collective-permute-done | bytes 8224 | tf_op jit(solution)/shard_map/ppermute | solution.py:28
  53.1 1.9 collective-permute-start.5
  55.2 65.8 %collective-permute-done.6 = f32[32,64]{1,0:T(8,128)S(1)} collective-permute-done((f32[32,64]{1,0:T(8,128)S(1)}, f32[32,64]{1,0:T(8,128)S(1)}, u32[]{:S(2)}, u32[]{:S(2)}) %collective-permute-start.6) | collective-permute-done | bytes 8224 | tf_op jit(solution)/shard_map/ppermute | solution.py:34
  120.9 6.6 %collective-permute-start.10 = (f32[32,64]{1,0:T(8,128)S(1)}, f32[32,64]{1,0:T(8,128)S(1)}, u32[]{:S(2)}, u32[]{:S(2)}) collective-permute-start(f32[32,64]{1,0:T(8,128)S(1)} %fusion.140), channel_id=1, source_target_pairs={{0,4},{1,5},{2,6},{3,7},{4,0},{5,1},{6,2},{7,3},{8,12},{9,13},{10,... | collective-permute-start | bytes 24584 | tf_op jit(solution)/shard_map/ppermute | solution.py:28
  128.4 6.7 %collective-permute-start.9 = (f32[32,64]{1,0:T(8,128)S(1)}, f32[32,64]{1,0:T(8,128)S(1)}, u32[]{:S(2)}, u32[]{:S(2)}) collective-permute-start(f32[32,64]{1,0:T(8,128)S(1)} %select_add_fusion.1), channel_id=1, source_target_pairs={{8,0},{9,1},{10,2},{11,3},{12,4},{13,5},{14,6},{15,7},{16,8},{17,9... | collective-permute-start | bytes 24584 | tf_op jit(solution)/shard_map/ppermute | solution.py:34
  135.0 1.4 collective-permute-done.9
  136.4 8.9 %collective-permute-start.12 = (f32[32,64]{1,0:T(8,128)S(1)}, f32[32,64]{1,0:T(8,128)S(1)}, u32[]{:S(2)}, u32[]{:S(2)}) collective-permute-start(f32[32,64]{1,0:T(8,128)S(1)} %select_add_fusion), channel_id=1, source_target_pairs={{16,0},{17,1},{18,2},{19,3},{20,4},{21,5},{22,6},{23,7},{24,8},{25... | collective-permute-start | bytes 24584 | tf_op jit(solution)/shard_map/ppermute | solution.py:34
  146.8 1.9 collective-permute-start.11
  148.8 8.1 %collective-permute-done.11 = f32[32,64]{1,0:T(8,128)S(1)} collective-permute-done((f32[32,64]{1,0:T(8,128)S(1)}, f32[32,64]{1,0:T(8,128)S(1)}, u32[]{:S(2)}, u32[]{:S(2)}) %collective-permute-start.11) | collective-permute-done | bytes 8224 | tf_op jit(solution)/shard_map/ppermute | solution.py:34
  156.9 1.9 collective-permute-start.8
  159.1 6.7 %collective-permute-done.8 = f32[32,64]{1,0:T(8,128)S(1)} collective-permute-done((f32[32,64]{1,0:T(8,128)S(1)}, f32[32,64]{1,0:T(8,128)S(1)}, u32[]{:S(2)}, u32[]{:S(2)}) %collective-permute-start.8) | collective-permute-done | bytes 8224 | tf_op jit(solution)/shard_map/ppermute | solution.py:34
  167.9 2.7 %convolution_multiply_fusion.7 = f32[8,256,32]{1,2,0:T(8,128)S(1)} fusion(f32[8,256]{1,0:T(8,128)S(1)} %sub.188, f32[8,256]{1,0:T(8,128)S(1)} %sub.186, f32[8,256]{1,0:T(8,128)S(1)} %sub.183, f32[8,256]{1,0:T(8,128)S(1)} %sub.181, f32[8,256]{1,0:T(8,128)S(1)} %sub.178, f32[8,256]{1,0:T(8,128)S(1)} %sub.176, f32[8,256]{1,0:T(8,128)S(1)} %mul.326, ...), kind=kOutput, calls=%fused_computation.28 | convolution fusion | flops 40960000 | bytes 458784 | tf_op jit(solution)/shard_map/rjl,jil->rji/dot_general | solution.py:87
  170.5 2.6 %fusion.8 = f32[8,256,32]{1,2,0:T(8,128)S(1)} fusion(f32[8,256,32]{1,2,0:T(8,128)S(1)} %convolution_multiply_fusion.7, f32[8,256]{1,0:T(8,128)S(1)} %sub.388, f32[8,256]{1,0:T(8,128)S(1)} %sub.385, f32[8,256]{1,0:T(8,128)S(1)} %sub.382, f32[8,256]{1,0:T(8,128)S(1)} %mul.337, f32[8,256]{1,0:T(8,128)S(1)} %sub.186, f32[8,256]{1,0:T(8,128)S(1)} %sub.181, ...), kind=kOutput, calls=%fused_computation.27 | convolution fusion | flops 41025536 | bytes 720928 | tf_op jit(solution)/shard_map/rjl,jil->rji/dot_general | solution.py:87
  173.2 2.6 %fusion.7 = f32[8,256,32]{1,2,0:T(8,128)S(1)} fusion(f32[8,256,32]{1,2,0:T(8,128)S(1)} %fusion.8, f32[8,256]{1,0:T(8,128)S(1)} %sub.397, f32[8,256]{1,0:T(8,128)S(1)} %sub.394, f32[8,256]{1,0:T(8,128)S(1)} %sub.391, f32[8,256]{1,0:T(8,128)S(1)} %mul.346, f32[8,256]{1,0:T(8,128)S(1)} %sub.186, f32[8,256]{1,0:T(8,128)S(1)} %sub.181, f32[8,256]{1,0:T(8,128)S(1)} %sub.176, ...), kind=kOutput, calls=%fused_computation.25 | convolution fusion | flops 41025536 | bytes 720928 | tf_op jit(solution)/shard_map/rjl,jil->rji/dot_general | solution.py:87
  175.8 2.6 %fusion.6 = f32[8,256,32]{1,2,0:T(8,128)S(1)} fusion(f32[8,256,32]{1,2,0:T(8,128)S(1)} %fusion.7, f32[8,256]{1,0:T(8,128)S(1)} %sub.406, f32[8,256]{1,0:T(8,128)S(1)} %sub.403, f32[8,256]{1,0:T(8,128)S(1)} %sub.400, f32[8,256]{1,0:T(8,128)S(1)} %mul.355, f32[8,256]{1,0:T(8,128)S(1)} %sub.186, f32[8,256]{1,0:T(8,128)S(1)} %sub.181, f32[8,256]{1,0:T(8,128)S(1)} %sub.176, ...), kind=kOutput, calls=%fused_computation.23 | convolution fusion | flops 41025536 | bytes 720928 | tf_op jit(solution)/shard_map/rjl,jil->rji/dot_general | solution.py:87
  178.4 2.6 %convolution_add_fusion = f32[8,256,32]{1,2,0:T(8,128)S(1)} fusion(f32[8,256,32]{1,2,0:T(8,128)S(1)} %fusion.6, f32[8,256]{1,0:T(8,128)S(1)} %sub.186, f32[8,256]{1,0:T(8,128)S(1)} %sub.181, f32[8,256]{1,0:T(8,128)S(1)} %sub.176, f32[8,256]{1,0:T(8,128)S(1)} %mul.324, bf16[4,8,8,256]{3,2,1,0:T(8,128)(2,1)S(1)} %bitcast.129), kind=kOutput, calls=%fused_computation.21 | convolution fusion | flops 40435712 | bytes 688128 | tf_op jit(solution)/shard_map/rjl,jil->rji/dot_general | solution.py:87
  181.1 2.6 %fusion.5 = f32[8,256,32]{1,2,0:T(8,128)S(1)} fusion(f32[8,256,32]{1,2,0:T(8,128)S(1)} %convolution_add_fusion, f32[8,256]{1,0:T(8,128)S(1)} %sub.421, f32[8,256]{1,0:T(8,128)S(1)} %sub.418, f32[8,256]{1,0:T(8,128)S(1)} %sub.415, f32[8,256]{1,0:T(8,128)S(1)} %mul.370, f32[8,256]{1,0:T(8,128)S(1)} %sub.186, f32[8,256]{1,0:T(8,128)S(1)} %sub.181, ...), kind=kOutput, calls=%fused_computation.20 | convolution fusion | flops 41025536 | bytes 720928 | tf_op jit(solution)/shard_map/rjl,jil->rji/dot_general | solution.py:87
  183.7 2.6 %fusion.4 = f32[8,256,32]{1,2,0:T(8,128)S(1)} fusion(f32[8,256,32]{1,2,0:T(8,128)S(1)} %fusion.5, f32[8,256]{1,0:T(8,128)S(1)} %sub.430, f32[8,256]{1,0:T(8,128)S(1)} %sub.427, f32[8,256]{1,0:T(8,128)S(1)} %sub.424, f32[8,256]{1,0:T(8,128)S(1)} %mul.380, f32[8,256]{1,0:T(8,128)S(1)} %sub.186, f32[8,256]{1,0:T(8,128)S(1)} %sub.181, f32[8,256]{1,0:T(8,128)S(1)} %sub.176, ...), kind=kOutput, calls=%fused_computation.18 | convolution fusion | flops 41025536 | bytes 720928 | tf_op jit(solution)/shard_map/rjl,jil->rji/dot_general | solution.py:87
  186.4 2.6 %fusion.3 = f32[8,256,32]{1,2,0:T(8,128)S(1)} fusion(f32[8,256,32]{1,2,0:T(8,128)S(1)} %fusion.4, f32[8,256]{1,0:T(8,128)S(1)} %sub.439, f32[8,256]{1,0:T(8,128)S(1)} %sub.436, f32[8,256]{1,0:T(8,128)S(1)} %sub.433, f32[8,256]{1,0:T(8,128)S(1)} %mul.390, f32[8,256]{1,0:T(8,128)S(1)} %sub.186, f32[8,256]{1,0:T(8,128)S(1)} %sub.181, f32[8,256]{1,0:T(8,128)S(1)} %sub.176, ...), kind=kOutput, calls=%fused_computation.16 | convolution fusion | flops 41025536 | bytes 720928 | tf_op jit(solution)/shard_map/rjl,jil->rji/dot_general | solution.py:87
  189.0 2.7 %fusion.2 = f32[32,8,256]{2,0,1:T(8,128)} fusion(f32[8,256,32]{1,2,0:T(8,128)S(1)} %fusion.3, f32[8,256]{1,0:T(8,128)S(1)} %sub.448, f32[8,256]{1,0:T(8,128)S(1)} %sub.445, f32[8,256]{1,0:T(8,128)S(1)} %sub.442, f32[8,256]{1,0:T(8,128)S(1)} %mul.400, f32[8,256]{1,0:T(8,128)S(1)} %sub.186, f32[8,256]{1,0:T(8,128)S(1)} %sub.181, f32[8,256]{1,0:T(8,128)S(1)} %sub.176, ...), kind=kOutput, calls=%fused_computation.14 | convolution fusion | flops 41025536 | bytes 720928 | tf_op jit(solution)/shard_map/rjl,jil->rji/dot_general | solution.py:87
  191.7 5.1 %gather_fusion = bf16[256,2048]{1,0:T(8,128)(2,1)S(1)} fusion(bf16[1024,2048]{1,0:T(8,128)(2,1)} %bitcast.1, s32[1024]{0:T(1024)S(1)} %pad_clamp_fusion), kind=kCustom, calls=%fused_computation | custom fusion | bytes 2098176 | tf_op jit(solution)/shard_map/gather | solution.py:107
  196.8 2.2 %reshape.389 = bf16[8,32,32,64]{3,2,1,0:T(8,128)(2,1)S(1)} reshape(bf16[256,2048]{1,0:T(8,128)(2,1)S(1)} %gather_fusion) | data formatting | bytes 2097152 | tf_op jit(solution)/shard_map/reshape | solution.py:108
  199.0 3.0 %convolution_bitcast_fusion.1 = f32[8,32,64]{2,1,0:T(8,128)S(1)} fusion(bf16[8,32,32,64]{3,2,1,0:T(8,128)(2,1)S(1)} %reshape.389, bf16[8,32,64,64]{3,2,1,0:T(8,128)(2,1)} %param.15), kind=kOutput, calls=%fused_computation.31 | convolution fusion | flops 67108864 | bytes 3211264 | tf_op jit(solution)/shard_map/jcrk,jckm->jrm/dot_general | solution.py:109
  (111 shorter events, 10.5 us)
Async XLA Ops:
  0.0 1.0 copy-start
  3.2 42.8 %collective-permute-start.3 = (f32[32,64]{1,0:T(8,128)S(1)}, f32[32,64]{1,0:T(8,128)S(1)}, u32[]{:S(2)}, u32[]{:S(2)}) collective-permute-start(f32[32,64]{1,0:T(8,128)S(1)} %convolution_bitcast_fusion.3), channel_id=1, source_target_pairs={{2,0},{3,1},{4,2},{5,3},{6,4},{7,5},{8,6},{9,7},{10,8},{11,9},{12,... | collective-permute-start | bytes 24584 | tf_op jit(solution)/shard_map/ppermute | solution.py:34
  9.5 156.9 %collective-permute-start.2 = (f32[32,64]{1,0:T(8,128)S(1)}, f32[32,64]{1,0:T(8,128)S(1)}, u32[]{:S(2)}, u32[]{:S(2)}) collective-permute-start(f32[32,64]{1,0:T(8,128)S(1)} %convolution_bitcast_fusion.3), channel_id=1, source_target_pairs={{0,2},{1,3},{2,4},{3,5},{4,6},{5,7},{6,8},{7,9},{8,10},{9,11},{10,... | collective-permute-start | bytes 24584 | tf_op jit(solution)/shard_map/ppermute | solution.py:34
  12.4 31.5 %collective-permute-start.4 = (f32[32,64]{1,0:T(8,128)S(1)}, f32[32,64]{1,0:T(8,128)S(1)}, u32[]{:S(2)}, u32[]{:S(2)}) collective-permute-start(f32[32,64]{1,0:T(8,128)S(1)} %fusion.154), channel_id=1, source_target_pairs={{0,1},{1,0},{2,3},{3,2},{4,5},{5,4},{6,7},{7,6},{8,9},{9,8},{10,11... | collective-permute-start | bytes 24584 | tf_op jit(solution)/shard_map/ppermute | solution.py:28
  17.5 14.8 %copy-start.1 = (bf16[32,2048]{1,0:T(8,128)(2,1)S(1)}, bf16[32,2048]{1,0:T(8,128)(2,1)}, u32[]{:S(2)}) copy-start(bf16[32,2048]{1,0:T(8,128)(2,1)} %param.9) | copy-start | bytes 393220
  17.5 14.8 %copy-start.5 = (bf16[4,2048]{1,0:T(4,128)(2,1)S(1)}, bf16[4,2048]{1,0:T(4,128)(2,1)}, u32[]{:S(2)}) copy-start(bf16[4,2048]{1,0:T(4,128)(2,1)} %param.10) | copy-start | bytes 49156
  17.5 25.9 %copy-start.6 = (s32[8,32]{1,0:T(8,128)S(1)}, s32[8,32]{1,0:T(8,128)}, u32[]{:S(2)}) copy-start(s32[8,32]{1,0:T(8,128)} %param.12) | copy-start | bytes 3076
  17.5 26.1 %copy-start.7 = (s32[8,4]{0,1:T(4,128)S(1)}, s32[8,4]{0,1:T(4,128)}, u32[]{:S(2)}) copy-start(s32[8,4]{0,1:T(4,128)} %param.11) | copy-start | bytes 388
  17.5 30.3 %copy-start.4 = (bf16[4,2,64,64]{3,2,1,0:T(8,128)(2,1)S(1)}, bf16[4,2,64,64]{3,2,1,0:T(8,128)(2,1)}, u32[]{:S(2)}) copy-start(bf16[4,2,64,64]{3,2,1,0:T(8,128)(2,1)} %param.17) | copy-start | bytes 196612
  17.6 174.1 %all-to-all-start = ((bf16[128,8,2048]{2,1,0:T(8,128)(2,1)}), bf16[128,8,2048]{2,1,0:T(8,128)(2,1)}, u32[]{:S(2)}, u32[]{:S(2)}) async-start(bf16[128,8,2048]{2,1,0:T(8,128)(2,1)} %stack.3), calls=%async_computation | async-start | bytes 8388608 | tf_op jit(solution)/shard_map/all_to_all | solution.py:105
  32.4 134.2 %collective-permute-start = (bf16[36,1024]{1,0:T(8,128)(2,1)S(1)}, bf16[36,1024]{1,0:T(8,128)(2,1)S(1)}, u32[]{:S(2)}, u32[]{:S(2)}) collective-permute-start(bf16[36,1024]{1,0:T(8,128)(2,1)S(1)} %get-tuple-element.74), channel_id=1, source_target_pairs={{0,1},{1,2},{2,3},{3,4},{4,5},{5,6},{6,7},{7,8},{8,9},{9,10},{10,1... | collective-permute-start | bytes 221192 | tf_op jit(solution)/shard_map/ppermute | solution.py:19
  34.8 131.8 %collective-permute-start.1 = (bf16[36,1024]{1,0:T(8,128)(2,1)S(1)}, bf16[36,1024]{1,0:T(8,128)(2,1)S(1)}, u32[]{:S(2)}, u32[]{:S(2)}) collective-permute-start(bf16[36,1024]{1,0:T(8,128)(2,1)S(1)} %get-tuple-element.73), channel_id=1, source_target_pairs={{1,0},{2,1},{3,2},{4,3},{5,4},{6,5},{7,6},{8,7},{9,8},{10,9},{11,1... | collective-permute-start | bytes 221192 | tf_op jit(solution)/shard_map/ppermute | solution.py:20
  43.9 77.1 %collective-permute-start.6 = (f32[32,64]{1,0:T(8,128)S(1)}, f32[32,64]{1,0:T(8,128)S(1)}, u32[]{:S(2)}, u32[]{:S(2)}) collective-permute-start(f32[32,64]{1,0:T(8,128)S(1)} %select_add_fusion.2), channel_id=1, source_target_pairs={{4,0},{5,1},{6,2},{7,3},{8,4},{9,5},{10,6},{11,7},{12,8},{13,9},{1... | collective-permute-start | bytes 24584 | tf_op jit(solution)/shard_map/ppermute | solution.py:34
  46.0 7.1 %collective-permute-start.7 = (f32[32,64]{1,0:T(8,128)S(1)}, f32[32,64]{1,0:T(8,128)S(1)}, u32[]{:S(2)}, u32[]{:S(2)}) collective-permute-start(f32[32,64]{1,0:T(8,128)S(1)} %fusion.147), channel_id=1, source_target_pairs={{0,2},{1,3},{2,0},{3,1},{4,6},{5,7},{6,4},{7,5},{8,10},{9,11},{10,... | collective-permute-start | bytes 24584 | tf_op jit(solution)/shard_map/ppermute | solution.py:28
  53.1 113.1 %collective-permute-start.5 = (f32[32,64]{1,0:T(8,128)S(1)}, f32[32,64]{1,0:T(8,128)S(1)}, u32[]{:S(2)}, u32[]{:S(2)}) collective-permute-start(f32[32,64]{1,0:T(8,128)S(1)} %select_add_fusion.2), channel_id=1, source_target_pairs={{0,4},{1,5},{2,6},{3,7},{4,8},{5,9},{6,10},{7,11},{8,12},{9,13},{1... | collective-permute-start | bytes 24584 | tf_op jit(solution)/shard_map/ppermute | solution.py:34
  120.9 7.4 %collective-permute-start.10 = (f32[32,64]{1,0:T(8,128)S(1)}, f32[32,64]{1,0:T(8,128)S(1)}, u32[]{:S(2)}, u32[]{:S(2)}) collective-permute-start(f32[32,64]{1,0:T(8,128)S(1)} %fusion.140), channel_id=1, source_target_pairs={{0,4},{1,5},{2,6},{3,7},{4,0},{5,1},{6,2},{7,3},{8,12},{9,13},{10,... | collective-permute-start | bytes 24584 | tf_op jit(solution)/shard_map/ppermute | solution.py:28
  128.4 8.1 %collective-permute-start.9 = (f32[32,64]{1,0:T(8,128)S(1)}, f32[32,64]{1,0:T(8,128)S(1)}, u32[]{:S(2)}, u32[]{:S(2)}) collective-permute-start(f32[32,64]{1,0:T(8,128)S(1)} %select_add_fusion.1), channel_id=1, source_target_pairs={{8,0},{9,1},{10,2},{11,3},{12,4},{13,5},{14,6},{15,7},{16,8},{17,9... | collective-permute-start | bytes 24584 | tf_op jit(solution)/shard_map/ppermute | solution.py:34
  136.4 10.4 %collective-permute-start.12 = (f32[32,64]{1,0:T(8,128)S(1)}, f32[32,64]{1,0:T(8,128)S(1)}, u32[]{:S(2)}, u32[]{:S(2)}) collective-permute-start(f32[32,64]{1,0:T(8,128)S(1)} %select_add_fusion), channel_id=1, source_target_pairs={{16,0},{17,1},{18,2},{19,3},{20,4},{21,5},{22,6},{23,7},{24,8},{25... | collective-permute-start | bytes 24584 | tf_op jit(solution)/shard_map/ppermute | solution.py:34
  146.8 10.1 %collective-permute-start.11 = (f32[32,64]{1,0:T(8,128)S(1)}, f32[32,64]{1,0:T(8,128)S(1)}, u32[]{:S(2)}, u32[]{:S(2)}) collective-permute-start(f32[32,64]{1,0:T(8,128)S(1)} %select_add_fusion), channel_id=1, source_target_pairs={{0,16},{1,17},{2,18},{3,19},{4,20},{5,21},{6,22},{7,23},{8,24},{9,... | collective-permute-start | bytes 24584 | tf_op jit(solution)/shard_map/ppermute | solution.py:34
  156.9 8.9 %collective-permute-start.8 = (f32[32,64]{1,0:T(8,128)S(1)}, f32[32,64]{1,0:T(8,128)S(1)}, u32[]{:S(2)}, u32[]{:S(2)}) collective-permute-start(f32[32,64]{1,0:T(8,128)S(1)} %select_add_fusion.1), channel_id=1, source_target_pairs={{0,8},{1,9},{2,10},{3,11},{4,12},{5,13},{6,14},{7,15},{8,16},{9,17... | collective-permute-start | bytes 24584 | tf_op jit(solution)/shard_map/ppermute | solution.py:34
  199.0 3.1 %copy-start.2 = (bf16[8,64,64]{2,1,0:T(8,128)(2,1)S(1)}, bf16[8,64,64]{2,1,0:T(8,128)(2,1)}, u32[]{:S(2)}) copy-start(bf16[8,64,64]{2,1,0:T(8,128)(2,1)} %param.14) | copy-start | bytes 196612
  199.0 3.5 %copy-start.3 = (f32[32,8,256]{2,0,1:T(8,128)S(1)}, f32[32,8,256]{2,0,1:T(8,128)}, u32[]{:S(2)}) copy-start(f32[32,8,256]{2,0,1:T(8,128)} %fusion.2) | copy-start | bytes 786436
